TPU v7x, 256 devices: a whole 4x4x8 slice. The times are simulated.
256 devices in a mesh: col: 4 (over x_hi, core), grp: 64 (over y, x_lo, z).
Axes of the slice: x: 4 (x_hi: 2, x_lo: 2; x = x_hi * 2 + x_lo), y: 4, z: 8, core: 2. Of those that a mesh axis runs over, the one named last changes fastest.
Arguments:
- rows: float32 [4, 32768, 1024], P(None, 'grp', 'col'), may hold values from -6 to 6
- bag_ids: int32 [65536, 4, 16], P('grp'), may hold values from 0 to 511
- bag_lengths: int32 [65536, 4], P('grp'), may hold values from 1 to 16, as said below
- labels: int32 [65536], P('grp'), may hold values 0 or 1
- proj_weight: bfloat16 [4096, 256], replicated, may hold values from -0.09375 to 0.09375
- hidden_weight: bfloat16 [256, 1024], replicated, may hold values from -0.375 to 0.375
- hidden_bias: float32 [1024], replicated, may hold values from -3 to 3
- out_weight: float32 [1024], replicated, may hold values from -0.5 to 0.5
Outputs:
- row_grad: float32 [4, 32768, 1024], P(None, 'grp', 'col')
- proj_grad: float32 [4096, 256], P(('col', 'grp'))
- hidden_grad: float32 [256, 1024], replicated
- bias_grad: float32 [1024], replicated
- out_grad: float32 [1024], replicated
Inputs may be any that keep to these rules, and one draw needn't show every extreme that they name: `bag_lengths`: some sample has exactly 16 live lookups in some table.
All inputs are finite; a program needn't handle non-finite values. No bound on the sum of `labels` on one device may be relied on, other than what follows from the above.
Results may differ from a plain program's by a relative error of at most 0.0071.
Values may be sent and summed in bfloat16 or wider, within the bound.
A program may use at most 64 MiB of HBM per device.

v0:
```python
import jax
import jax.numpy as jnp
from jax import lax
from jax.sharding import PartitionSpec as P


def bag_counts(bag_row, bag_len, row_total):
    in_bag = jnp.arange(bag_row.shape[1], dtype=jnp.int32)[None, :] < bag_len[:, None]
    matches = (
        bag_row[:, :, None] == jnp.arange(row_total, dtype=jnp.int32)[None, None, :]
    ) & in_bag[:, :, None]
    return jnp.sum(matches.astype(jnp.float32), axis=1)


def contract_first(left, right):
    return lax.dot_general(
        left, right, (((0,), (0,)), ((), ())), preferred_element_type=jnp.float32
    )


def contract_last(left, right):
    return lax.dot_general(
        left, right, (((1,), (1,)), ((), ())), preferred_element_type=jnp.float32
    )


def body(rows, bag_ids, bag_lengths, labels, proj_weight, hidden_weight, hidden_bias, out_weight):
    n_slices = lax.axis_size("col")
    column_idx = lax.axis_index("col")
    tables = rows.shape[0]
    row_total = rows.shape[1]
    slice_width = rows.shape[2]
    samples = bag_ids.shape[0]
    own_rows = samples // n_slices
    counts = [
        bag_counts(bag_ids[:, table], bag_lengths[:, table], row_total) for table in range(tables)
    ]

    def pool_table(table):
        return jnp.dot(counts[table], rows[table], precision=lax.Precision.HIGHEST).astype(
            jnp.bfloat16
        )

    own_labels = lax.dynamic_slice_in_dim(labels, column_idx * own_rows, own_rows, 0).astype(
        jnp.float32
    )
    pooled = jnp.concatenate([pool_table(table) for table in range(tables)], axis=1)
    features = lax.all_to_all(pooled, "col", split_axis=0, concat_axis=1, tiled=True)
    projected = jnp.dot(features, proj_weight, preferred_element_type=jnp.float32).astype(
        jnp.bfloat16
    )
    hidden_pre = jnp.dot(projected, hidden_weight, preferred_element_type=jnp.float32) + hidden_bias
    sig_pre = jax.nn.sigmoid(hidden_pre)
    active = hidden_pre * sig_pre
    logits = jnp.sum(active * out_weight, axis=1)
    slopes = jax.nn.sigmoid(logits) - own_labels
    d_hidden = slopes[:, None] * out_weight * (sig_pre * (1.0 + hidden_pre * (1.0 - sig_pre)))
    d_hidden_b = d_hidden.astype(jnp.bfloat16)
    dense_grads = (
        contract_first(projected, d_hidden_b),
        jnp.sum(d_hidden, axis=0),
        jnp.sum(active * slopes[:, None], axis=0),
    )
    top_d_projected = contract_last(d_hidden_b, hidden_weight).astype(jnp.bfloat16)
    d_projected, dense_grads = (top_d_projected, dense_grads)
    proj_grad = lax.psum_scatter(
        contract_first(features, d_projected), ("col", "grp"), scatter_dimension=0, tiled=True
    )
    d_features = contract_last(d_projected, proj_weight).astype(jnp.bfloat16)
    d_features = d_features.reshape(own_rows, n_slices, tables * slice_width)
    returned = lax.all_to_all(d_features, "col", split_axis=1, concat_axis=0, tiled=True).reshape(
        samples, tables, slice_width
    )
    hidden_grad, bias_grad, out_grad = lax.psum(
        (dense_grads[0], dense_grads[1], dense_grads[2]), ("col", "grp")
    )
    row_grad = jnp.stack(
        [
            contract_first(counts[table].astype(jnp.bfloat16), returned[:, table])
            for table in range(tables)
        ]
    )
    return (row_grad, proj_grad, hidden_grad, bias_grad, out_grad)


def solution(mesh):
    return jax.shard_map(
        body,
        mesh=mesh,
        in_specs=(
            P(None, "grp", "col"),
            P("grp", None, None),
            P("grp", None),
            P("grp"),
            P(),
            P(),
            P(),
            P(),
        ),
        out_specs=(P(None, "grp", "col"), P(("col", "grp"), None), P(), P(), P()),
        check_vma=False,
    )
```

profile of v0, /device:TPU:0, one launch (start us, length us, event | category | flops | bytes accessed | tf_op | source)
XLA Modules:
  0.0 1657.6 jit_solution(7463367642675961723)
XLA Ops:
  7.2 0.0 copy-start
  7.2 1.1 slice_bitcast_fusion.3
  8.3 0.2 copy.26
  8.5 0.9 fusion.30
  9.4 0.2 iota_compare_fusion.4
  9.6 0.2 copy.25
  9.8 0.0 copy-start.9
  9.8 0.2 iota_compare_fusion.5
  10.0 10.5 convert_reduce_fusion
  20.5 0.0 copy-done.9
  20.5 0.0 copy-start.1
  20.5 2.9 convolution_convert_fusion.1
  23.4 10.5 convert_reduce_fusion.1
  33.8 2.1 convolution_convert_fusion.2
  35.9 0.2 copy.24
  36.1 0.2 iota_compare_fusion.6
  36.3 10.5 convert_reduce_fusion.2
  46.8 1.3 copy-done.5
  48.2 3.8 convolution_convert_fusion.3
  52.0 0.2 copy.23
  52.2 0.2 iota_compare_fusion.7
  52.4 10.6 convert_reduce_fusion.3
  63.1 0.0 copy-start.10
  63.1 0.0 copy-start.11
  63.1 3.5 convolution_convert_fusion.4
  66.6 0.0 copy-done.10
  66.6 0.0 copy-done.11
  66.6 0.2 pad_maximum_fusion
  66.8 1.5 copy.54
  68.3 4.5 all-to-all-start
  72.8 0.0 all-reduce.3.cloned.1.call-start
  72.8 27.2 %all-to-all-done = bf16[4,256,1024]{1,2,0:T(8,128)(2,1)} async-done(((bf16[4,256,1024]{1,2,0:T(8,128)(2,1)}), bf16[4,256,1024]{1,2,0:T(8,128)(2,1)}, u32[]{:S(2)}, u32[]{:S(2)}) %all-to-all-start) | async-done | bytes 2097184 | tf_op jit(solution)/shard_map/all_to_all | solution.py:48
  100.1 2.4 convolution_convert_fusion.6
  102.5 0.0 copy-done.12
  102.5 0.0 copy-done.13
  102.5 0.0 copy-done.14
  102.5 0.6 multiply_reduce_fusion.1
  103.1 0.8 divide_subtract_fusion
  103.8 0.6 fusion.28
  104.4 1.3 fusion.25
  105.7 0.0 all-reduce.3.cloned.1.call-update
  105.7 0.0 reduce-scatter.2.cloned.1.call-start
  105.8 0.3 convolution_convert_fusion.5
  106.1 4.2 fusion.31
  110.4 0.0 reduce-scatter.2.cloned.1.call-update
  110.4 0.7 convolution_convert_fusion
  111.2 1.5 copy.53
  112.7 4.5 all-to-all-start.1
  117.2 96.8 %all-reduce = (f32[1024]{0:T(1024)}, f32[1024]{0:T(1024)}) all-reduce(f32[1024]{0:T(1024)S(1)} %get-tuple-element.7, f32[1024]{0:T(1024)S(1)} %get-tuple-element.13), channel_id=1, replica_groups=mesh['col'=4,'grp'=64] {'col','grp'}, use_global_device_ids=true, to_apply=%region_8.0 | all-reduce | flops 2048 | bytes 16384 | tf_op jit(solution)/shard_map/psum | solution.py:74
  214.0 0.0 all-to-all-done.1
  214.0 4.5 reshape.116
  218.5 8.2 fusion.29
  226.7 0.5 convolution_bitcast_fusion.3
  227.2 1.1 copy-done.6
  228.3 0.5 convolution_bitcast_fusion.2
  228.7 0.0 copy-start.2
  228.7 0.3 copy-done.4
  229.0 0.5 convolution_bitcast_fusion.1
  229.5 0.9 copy-done.2
  230.4 0.5 convolution_bitcast_fusion
  230.9 1.5 pad_maximum_fusion.1
  232.4 136.6 %all-reduce.3.cloned.1.call-done = f32[256,1024]{1,0:T(8,128)} async-done(((f32[256,1024]{1,0:T(8,128)}), f32[256,1024]{1,0:T(8,128)}) %all-reduce.3.cloned.1.call-update) | async-done | bytes 1048592 | tf_op jit(solution)/shard_map/psum | solution.py:74
  369.0 1279.5 %reduce-scatter.2.cloned.1.call-done = f32[16,256]{1,0:T(8,128)} async-done(((f32[4096,256]{1,0:T(8,128)}), f32[16,256]{1,0:T(8,128)}) %reduce-scatter.2.cloned.1.call-update) | async-done | bytes 16400 | tf_op jit(solution)/shard_map/reduce_scatter | solution.py:66
  1648.5 2.3 copy.56
  (14 shorter events, 0.0 us)
Async XLA Ops:
  7.2 92.9 %copy-start = (bf16[4096,256]{1,0:T(8,128)(2,1)S(1)}, bf16[4096,256]{1,0:T(8,128)(2,1)}, u32[]{:S(2)}) copy-start(bf16[4096,256]{1,0:T(8,128)(2,1)} %param.12) | copy-start | bytes 6291460
  9.8 10.7 copy-start.9
  20.5 13.3 copy-start.1
  33.8 2.1 copy-start.3
  46.8 1.3 copy-start.5
  63.0 3.8 copy-start.7
  63.1 3.6 copy-start.10
  63.1 3.6 copy-start.11
  68.3 31.7 %all-to-all-start = ((bf16[4,256,1024]{1,2,0:T(8,128)(2,1)}), bf16[4,256,1024]{1,2,0:T(8,128)(2,1)}, u32[]{:S(2)}, u32[]{:S(2)}) async-start(bf16[4,256,1024]{1,2,0:T(8,128)(2,1)} %bitcast.78), calls=%async_computation | async-start | bytes 4194304 | tf_op jit(solution)/shard_map/all_to_all | solution.py:48
  72.8 296.2 %all-reduce.3.cloned.1.call-start = ((), (), s32[]{:S(2)}) async-start(), calls=%async_computation.4 | async-start | bytes 2097152 | tf_op jit(solution)/shard_map/psum | solution.py:74
  100.1 2.4 copy-start.12
  100.1 2.4 copy-start.13
  100.1 2.4 copy-start.14
  105.7 1542.7 %reduce-scatter.2.cloned.1.call-start = ((), (), s32[]{:S(2)}) async-start(), calls=%async_computation.3 | async-start | bytes 4210688 | tf_op jit(solution)/shard_map/reduce_scatter | solution.py:66
  112.7 101.3 %all-to-all-start.1 = ((bf16[256,4,1024]{2,0,1:T(8,128)(2,1)}), bf16[256,4,1024]{2,0,1:T(8,128)(2,1)}, u32[]{:S(2)}, u32[]{:S(2)}) async-start(bf16[256,4,1024]{2,0,1:T(8,128)(2,1)} %bitcast.79), calls=%async_computation.1 | async-start | bytes 4194304 | tf_op jit(solution)/shard_map/all_to_all | solution.py:71
  218.5 8.2 copy-start.8
  226.7 1.6 copy-start.6
  227.2 1.9 copy-start.4
  228.7 1.7 copy-start.2
Sparse Core Ops, SparseCore 0:
  105.9 263.0 all-reduce.2
  372.2 1276.2 reduce-scatter.1
where the time goes:
time: 1660 us
  waiting for transfers between devices  1440 us (87%)
  blocking collectives  96.8 us (6%)
  other arithmetic  45.9 us (3%)
  local copies, waits for them, and re-layouts  24.4 us (1%)
  matrix products  23.7 us (1%)
    reduce_scatter x1, waiting for transfers between devices, body(): lax.psum_scatter(contract_first(features, d_projected), ('col', 'grp'), s...  1280 us
    psum x1, waiting for transfers between devices, body(): lax.psum((dense_grads[0], dense_grads[1], dense_grads[2]), ('col', 'grp'))  137 us
    psum x1, blocking collectives, body(): lax.psum((dense_grads[0], dense_grads[1], dense_grads[2]), ('col', 'grp'))  96.8 us
    reduce_sum x4, other arithmetic, bag_counts(): return jnp.sum(matches.astype(jnp.float32), axis=1)  42 us
  transfers between devices with their start and end apart: 4, of which 3 were waited for; matrix products, arithmetic and copies ran while one was open for 1% of the time, Pallas kernels for 0%

commit v1 on v0

v1 whole, which is shorter than its diff:
```python
import jax
import jax.numpy as jnp
from jax import lax
from jax.experimental import pallas as pl
from jax.experimental.pallas import tpu as pltpu
from jax.sharding import PartitionSpec as P

MESH = pl.DeviceIdType.MESH
BF = jnp.bfloat16
F32 = jnp.float32
NZ = 8
NP = 8
CH = 256


def mm(a, b):
    return lax.dot_general(a, b, (((1,), (0,)), ((), ())), preferred_element_type=F32)


def mm_nt(a, b):
    return lax.dot_general(a, b, (((1,), (1,)), ((), ())), preferred_element_type=F32)


def split_hi_lo(v):
    hi = v.astype(BF)
    return hi, (v - hi.astype(F32)).astype(BF)


def kernel(
    ids_ref, lens_ref, lab_ref, hw_ref, bias_ref, ow_ref, rows_hbm, pw_hbm,
    rg_hbm, proj_ref, hid_ref, bg_ref, og_ref,
    rows_ref, wc_ref, rt_ref, wct_ref, hwt_ref, bc_ref, oc_ref,
    cnt_ref, pool_ref, part_ref, ra_ref, sb_ref, rb_ref, pt_ref,
    gb_ref, act_ref, sl_ref, spt_ref, dpt_ref, dpool_ref, rg_ref,
    hs1_ref, hr1_ref, ps1_ref, pr1_ref, hs2_ref, hr2_ref, ps2_ref, pr2_ref,
    hs3_ref, hr3_ref, hr4_ref,
    in_sem, rg_sem, a_send, a_recv, b_send, b_recv, c_send, c_recv,
    h1_send, h1_recv, p1_send, p1_recv, h2_send, h2_recv, p2_send, p2_recv,
    h3_send, h3_recv, h4_send, h4_recv,
):
    c = lax.axis_index("col")
    g = lax.axis_index("grp")
    h, k = c // 2, lax.rem(c, 2)
    p, z = g // NZ, lax.rem(g, NZ)
    tables, _, samples = ids_ref.shape
    bag = ids_ref.shape[1]
    row_total = rows_ref.shape[1]
    width = rows_ref.shape[2]
    hid = hw_ref.shape[1]
    n_ch = samples // CH

    core_peer = {"col": 2 * h + (1 - k), "grp": g}
    chip_peer = {"col": 2 * (1 - h) + k, "grp": g}

    def plane_peer(d):
        q = lax.rem(p + d, NP)
        return q, {"col": c, "grp": q * NZ + z}

    def z_peer(d):
        q = lax.rem(z + d, NZ)
        return q, {"col": c, "grp": p * NZ + q}

    def far_peer(d):
        e = lax.rem(h * NP + p + d, 2 * NP)
        qh, qp = e // NP, lax.rem(e, NP)
        return e, {"col": 2 * qh + k, "grp": qp * NZ + z}

    def rows_copy(t):
        return pltpu.make_async_copy(rows_hbm.at[t], rows_ref.at[t], in_sem.at[t])

    w_copy = pltpu.make_async_copy(
        pw_hbm.at[pl.ds(pl.multiple_of(c * tables * width, 256), tables * width)], wc_ref, in_sem.at[tables]
    )
    for t in range(tables):
        rows_copy(t).start()
    w_copy.start()

    barrier = pltpu.get_barrier_semaphore()
    pl.semaphore_signal(barrier, inc=1, device_id=core_peer, device_id_type=MESH)

    def greet_far(d, carry):
        pl.semaphore_signal(barrier, inc=1, device_id=far_peer(d)[1], device_id_type=MESH)
        return carry

    def greet_z(d, carry):
        pl.semaphore_signal(barrier, inc=1, device_id=z_peer(d)[1], device_id_type=MESH)
        return carry

    lax.fori_loop(1, 2 * NP, greet_far, 0)
    lax.fori_loop(1, NZ, greet_z, 0)

    hwt_ref[...] = hw_ref[...].T
    bc_ref[...] = jnp.broadcast_to(bias_ref[...], (128, hid)).T
    oc_ref[...] = jnp.broadcast_to(ow_ref[...], (128, hid)).T
    for t in range(tables):
        rows_copy(t).wait()
        rt = rows_ref[t].T
        hi, lo = split_hi_lo(rt)
        rt_ref[t, :, :row_total] = hi
        rt_ref[t, :, row_total:] = lo
    w_copy.wait()
    wct_ref[...] = wc_ref[...].T
    pl.semaphore_wait(barrier, 2 * NP + NZ - 1)

    def cols_of(j):
        return pl.ds(pl.multiple_of(j * CH, CH), CH)

    def counts_block(j, i):
        t, b = i // 2, lax.rem(i, 2)
        cols = pl.ds(pl.multiple_of(j * CH + b * 128, 128), 128)
        ids = ids_ref[t, :, cols]
        spot = lax.broadcasted_iota(jnp.int32, (bag, 128), 0)
        ids = jnp.where(spot < lens_ref[t, :, cols], ids, -1)
        spread = [jnp.broadcast_to(ids[q : q + 1], (16, 128)).astype(jnp.int16) for q in range(bag)]
        first = lax.broadcasted_iota(jnp.int32, (16, 128), 0).astype(jnp.int16)
        one, zero = jnp.ones((16, 128), BF), jnp.zeros((16, 128), BF)
        for r in range(row_total // 16):
            row = first + jnp.int16(r * 16)
            acc = jnp.where(spread[0] == row, one, zero)
            for q in range(1, bag):
                acc = acc + jnp.where(spread[q] == row, one, zero)
            cnt_ref[t, r * 16 : (r + 1) * 16, cols] = acc

    own_half = pl.ds(pl.multiple_of(k * 128, 128), 128)
    other_half = pl.ds(pl.multiple_of((1 - k) * 128, 128), 128)

    def copy_a(j):
        return pltpu.make_async_remote_copy(
            part_ref.at[j, other_half], ra_ref.at[j], a_send.at[j], a_recv.at[j],
            device_id=core_peer, device_id_type=MESH)

    def copy_b(j):
        return pltpu.make_async_remote_copy(
            sb_ref.at[j], rb_ref.at[j], b_send.at[j], b_recv.at[j],
            device_id=chip_peer, device_id_type=MESH)

    def copy_c(j):
        return pltpu.make_async_remote_copy(
            pt_ref.at[j, own_half], pt_ref.at[j, own_half], c_send.at[j], c_recv.at[j],
            device_id=core_peer, device_id_type=MESH)

    def wait_c(j):
        pltpu.make_async_remote_copy(
            pt_ref.at[j, other_half], pt_ref.at[j, other_half], c_send.at[j], c_recv.at[j],
            device_id=core_peer, device_id_type=MESH).wait_recv()

    def chunk(j):
        cols = cols_of(j)

        def one_block(i, carry):
            counts_block(j, i)
            return carry

        lax.fori_loop(0, 2 * tables, one_block, 0)
        for t in range(tables):
            cnt = cnt_ref[t, :, cols]
            acc = mm(rt_ref[t, :, :row_total], cnt) + mm(rt_ref[t, :, row_total:], cnt)
            pool_ref[t * width : (t + 1) * width, cols] = acc.astype(BF)
        part_ref[j] = mm(wct_ref[...], pool_ref[:, cols])
        copy_a(j).start()

    def stage_b(j):
        copy_a(j).wait_recv()
        sb_ref[j] = (part_ref[j, own_half] + ra_ref[j]).astype(BF)
        copy_b(j).start()

    def stage_c(j):
        copy_b(j).wait_recv()
        pt_ref[j, own_half] = (sb_ref[j].astype(F32) + rb_ref[j].astype(F32)).astype(BF)
        copy_c(j).start()

    def mlp(j):
        wait_c(j)
        cols = cols_of(j)
        pt = pt_ref[j]
        logits = jnp.zeros((1, CH), F32)
        for q in range(hid // 256):
            hs = slice(q * 256, (q + 1) * 256)
            bias = jnp.concatenate([bc_ref[hs, :]] * (CH // 128), axis=1)
            ow = jnp.concatenate([oc_ref[hs, :]] * (CH // 128), axis=1)
            pre = mm(hwt_ref[hs, :], pt) + bias
            sig = 0.5 * jnp.tanh(0.5 * pre) + 0.5
            act = pre * sig
            logits = logits + jnp.sum(act * ow, axis=0, keepdims=True)
            gb_ref[hs, cols] = (ow * (sig + act * (1.0 - sig))).astype(BF)
            act_ref[hs, cols] = act.astype(BF)
        slopes = 0.5 * jnp.tanh(0.5 * logits) + 0.5 - lab_ref[:, cols].astype(F32)
        hi, lo = split_hi_lo(slopes)
        spot = lax.broadcasted_iota(jnp.int32, (16, CH), 0)
        sl_ref[:, cols] = jnp.where(
            spot == 0, hi.astype(F32), jnp.where(spot == 1, lo.astype(F32), 0.0)
        ).astype(BF)
        dpt_ref[:, cols] = (mm(hw_ref[...], gb_ref[:, cols]) * slopes).astype(BF)
        spt_ref[:, cols] = (pt.astype(F32) * slopes).astype(BF)

    for j in range(n_ch):
        chunk(j)
        if j >= 1:
            stage_b(j - 1)
        if j >= 2:
            stage_c(j - 2)
    stage_b(n_ch - 1)
    mlp(0)
    stage_c(n_ch - 2)
    mlp(1)
    stage_c(n_ch - 1)
    mlp(2)
    mlp(3)

    hs = pl.ds(pl.multiple_of(c * 256, 256), 256)
    g_own = gb_ref[hs, :]
    hgrad = mm_nt(spt_ref[...], g_own)
    brow = mm_nt(sl_ref[...], g_own)
    orow = mm_nt(sl_ref[...], act_ref[hs, :])

    def vec_rows(bias_row, out_row):
        bh, bl = split_hi_lo(bias_row)
        oh, ol = split_hi_lo(out_row)
        spot = lax.broadcasted_iota(jnp.int32, (16, 256), 0)
        out = jnp.zeros((16, 256), F32)
        for place, v in enumerate((bh, bl, oh, ol)):
            out = jnp.where(spot == place, v.astype(F32), out)
        return out.astype(BF)

    vec = vec_rows(brow[0:1] + brow[1:2], orow[0:1] + orow[1:2])
    for q in range(NP):
        hs1_ref[q, :32] = hgrad[q * 32 : (q + 1) * 32].astype(BF)
        hs1_ref[q, 32:] = vec

    def h1_copy(q, dev):
        return pltpu.make_async_remote_copy(
            hs1_ref.at[q], hr1_ref.at[p], h1_send.at[q], h1_recv.at[p], device_id=dev, device_id_type=MESH)

    def p1_copy(q, dev):
        return pltpu.make_async_remote_copy(
            ps1_ref.at[q], pr1_ref.at[p], p1_send.at[q], p1_recv.at[p], device_id=dev, device_id_type=MESH)

    def h2_copy(q, dev):
        return pltpu.make_async_remote_copy(
            hs2_ref, hr2_ref.at[z], h2_send.at[q], h2_recv.at[z], device_id=dev, device_id_type=MESH)

    def p2_copy(q, dev):
        return pltpu.make_async_remote_copy(
            ps2_ref.at[q], pr2_ref.at[z], p2_send.at[q], p2_recv.at[z], device_id=dev, device_id_type=MESH)

    def h3_copy(e, dev):
        own = h * NP + p
        return pltpu.make_async_remote_copy(
            hs3_ref, hr3_ref.at[own], h3_send.at[e], h3_recv.at[own], device_id=dev, device_id_type=MESH)

    def start_all(peer, copy, count):
        def go(d, carry):
            copy(*peer(d)).start()
            return carry

        lax.fori_loop(1, count, go, 0)

    def wait_all(peer, src, dst_slots, send, recv, count):
        def go(d, carry):
            q, dev = peer(d)
            pltpu.make_async_remote_copy(
                src(q), dst_slots.at[q], send.at[q], recv.at[q], device_id=dev, device_id_type=MESH).wait_recv()
            return carry

        lax.fori_loop(1, count, go, 0)

    def wait_sent(peer, copy, count):
        def go(d, carry):
            copy(*peer(d)).wait_send()
            return carry

        lax.fori_loop(1, count, go, 0)

    start_all(plane_peer, h1_copy, NP)
    hr1_ref[p] = hs1_ref[p]

    for t in range(tables):
        pg = mm_nt(pool_ref[t * width : (t + 1) * width], dpt_ref[...])
        half = NP // tables
        for q in range(half):
            ps1_ref[t * half + q] = pg[q * 128 : (q + 1) * 128].astype(BF)
    start_all(plane_peer, p1_copy, NP)
    pr1_ref[p] = ps1_ref[p]

    def row_grad(t):
        ws = slice(t * width, (t + 1) * width)
        dpool_ref[ws] = mm(wc_ref[ws], dpt_ref[...]).astype(BF)
        rg_ref[t] = mm_nt(cnt_ref[t], dpool_ref[ws])
        pltpu.make_async_copy(rg_ref.at[t], rg_hbm.at[t], rg_sem.at[t]).start()

    def slot_sum(ref, rows):
        acc = ref[0, rows].astype(F32)
        for q in range(1, NP):
            acc = acc + ref[q, rows].astype(F32)
        return acc

    row_grad(0)

    wait_all(plane_peer, lambda q: hs1_ref.at[q], hr1_ref, h1_send, h1_recv, NP)
    hs2_ref[:32] = slot_sum(hr1_ref, slice(0, 32)).astype(BF)
    v = slot_sum(hr1_ref, slice(32, 48))
    hs2_ref[32:] = vec_rows(v[0:1] + v[1:2], v[2:3] + v[3:4])
    start_all(z_peer, h2_copy, NZ)
    hr2_ref[z] = hs2_ref[...]

    row_grad(1)

    wait_all(plane_peer, lambda q: ps1_ref.at[q], pr1_ref, p1_send, p1_recv, NP)
    for q in range(NZ):
        ps2_ref[q] = slot_sum(pr1_ref, slice(q * 16, (q + 1) * 16)).astype(BF)
    start_all(z_peer, p2_copy, NZ)
    pr2_ref[z] = ps2_ref[z]

    wait_all(z_peer, lambda q: hs2_ref, hr2_ref, h2_send, h2_recv, NZ)
    hs3_ref[:32] = slot_sum(hr2_ref, slice(0, 32)).astype(BF)
    v = slot_sum(hr2_ref, slice(32, 48))
    hs3_ref[32:] = vec_rows(v[0:1] + v[1:2], v[2:3] + v[3:4])
    start_all(far_peer, h3_copy, 2 * NP)
    hr3_ref[h * NP + p] = hs3_ref[...]

    row_grad(2)
    row_grad(3)

    wait_all(z_peer, lambda q: ps2_ref.at[q], pr2_ref, p2_send, p2_recv, NZ)
    proj_ref[...] = slot_sum(pr2_ref, slice(0, 16))

    wait_all(far_peer, lambda e: hs3_ref, hr3_ref, h3_send, h3_recv, 2 * NP)
    h4 = pltpu.make_async_remote_copy(
        hr3_ref, hr4_ref, h4_send, h4_recv, device_id=core_peer, device_id_type=MESH)
    h4.start()

    def put(ref, core):
        for qh in range(2):
            col = pl.ds(pl.multiple_of((2 * qh + core) * 256, 256), 256)
            for q in range(NP):
                hid_ref[q * 32 : (q + 1) * 32, col] = ref[qh * NP + q, :32].astype(F32)
            v = ref[qh * NP, 32:].astype(F32)
            bg_ref[:, col] = v[0:1] + v[1:2]
            og_ref[:, col] = v[2:3] + v[3:4]

    put(hr3_ref, k)
    h4.wait()
    put(hr4_ref, 1 - k)

    for j in range(n_ch):
        copy_a(j).wait_send()
        copy_b(j).wait_send()
        copy_c(j).wait_send()
    wait_sent(plane_peer, h1_copy, NP)
    wait_sent(plane_peer, p1_copy, NP)
    wait_sent(z_peer, h2_copy, NZ)
    wait_sent(z_peer, p2_copy, NZ)
    wait_sent(far_peer, h3_copy, 2 * NP)
    for t in range(tables):
        pltpu.make_async_copy(rg_ref.at[t], rg_hbm.at[t], rg_sem.at[t]).wait()


def body(rows, bag_ids, bag_lengths, labels, proj_weight, hidden_weight, hidden_bias, out_weight):
    tables, row_total, width = rows.shape
    samples, _, bag = bag_ids.shape
    feats, proj = proj_weight.shape
    hid = hidden_weight.shape[1]
    own = tables * width
    n_ch = samples // CH
    ids = bag_ids.transpose(1, 2, 0)
    lens = bag_lengths.T.reshape(tables, 1, samples)
    vm = pl.BlockSpec(memory_space=pltpu.VMEM)
    hbm = pl.BlockSpec(memory_space=pl.ANY)
    dma = pltpu.SemaphoreType.DMA
    out = pl.pallas_call(
        kernel,
        out_shape=(
            jax.ShapeDtypeStruct(rows.shape, F32),
            jax.ShapeDtypeStruct((feats // 256, proj), F32),
            jax.ShapeDtypeStruct((proj, hid), F32),
            jax.ShapeDtypeStruct((1, hid), F32),
            jax.ShapeDtypeStruct((1, hid), F32),
        ),
        in_specs=[vm] * 6 + [hbm] * 2,
        out_specs=(hbm, vm, vm, vm, vm),
        scratch_shapes=[
            pltpu.VMEM((tables, row_total, width), F32),
            pltpu.VMEM((own, proj), BF),
            pltpu.VMEM((tables, width, 2 * row_total), BF),
            pltpu.VMEM((proj, own), BF),
            pltpu.VMEM((hid, proj), BF),
            pltpu.VMEM((hid, 128), F32),
            pltpu.VMEM((hid, 128), F32),
            pltpu.VMEM((tables, row_total, samples), BF),
            pltpu.VMEM((own, samples), BF),
            pltpu.VMEM((n_ch, proj, CH), F32),
            pltpu.VMEM((n_ch, proj // 2, CH), F32),
            pltpu.VMEM((n_ch, proj // 2, CH), BF),
            pltpu.VMEM((n_ch, proj // 2, CH), BF),
            pltpu.VMEM((n_ch, proj, CH), BF),
            pltpu.VMEM((hid, samples), BF),
            pltpu.VMEM((hid, samples), BF),
            pltpu.VMEM((16, samples), BF),
            pltpu.VMEM((proj, samples), BF),
            pltpu.VMEM((proj, samples), BF),
            pltpu.VMEM((own, samples), BF),
            pltpu.VMEM((tables, row_total, width), F32),
            pltpu.VMEM((NP, 48, 256), BF),
            pltpu.VMEM((NP, 48, 256), BF),
            pltpu.VMEM((NP, 128, proj), BF),
            pltpu.VMEM((NP, 128, proj), BF),
            pltpu.VMEM((48, 256), BF),
            pltpu.VMEM((NZ, 48, 256), BF),
            pltpu.VMEM((NZ, 16, proj), BF),
            pltpu.VMEM((NZ, 16, proj), BF),
            pltpu.VMEM((48, 256), BF),
            pltpu.VMEM((2 * NP, 48, 256), BF),
            pltpu.VMEM((2 * NP, 48, 256), BF),
            dma((tables + 1,)),
            dma((tables,)),
            dma((n_ch,)), dma((n_ch,)), dma((n_ch,)), dma((n_ch,)), dma((n_ch,)), dma((n_ch,)),
            dma((NP,)), dma((NP,)), dma((NP,)), dma((NP,)),
            dma((NZ,)), dma((NZ,)), dma((NZ,)), dma((NZ,)),
            dma((2 * NP,)), dma((2 * NP,)),
            dma(()), dma(()),
        ],
        compiler_params=pltpu.CompilerParams(
            collective_id=0, has_side_effects=True, vmem_limit_bytes=52 * 1024 * 1024
        ),
    )(
        ids, lens, labels.reshape(1, samples), hidden_weight, hidden_bias.reshape(1, hid),
        out_weight.reshape(1, hid), rows, proj_weight,
    )
    return out[0], out[1], out[2], out[3].reshape(hid), out[4].reshape(hid)


def solution(mesh):
    return jax.shard_map(
        body,
        mesh=mesh,
        in_specs=(
            P(None, "grp", "col"),
            P("grp", None, None),
            P("grp", None),
            P("grp"),
            P(),
            P(),
            P(),
            P(),
        ),
        out_specs=(P(None, "grp", "col"), P(("col", "grp"), None), P(), P(), P()),
        check_vma=False,
    )
```

time: 1660 us -> 64.6 us (0.04)
  the two profiles are of different devices: /device:TPU:0 before, /device:TPU:1 now
where the time goes in v1:
time: 64.6 us; the launch traced here: 64.2 us
  Pallas kernels  53 us (82%)
  local copies, waits for them, and re-layouts  10.6 us (16%)
  between operations  0.66 us (1%)
    pallas_call x1, Pallas kernels, body(): pl.pallas_call(kernel, out_shape=(jax.ShapeDtypeStruct(rows.shape, F32),...  53 us
    unnamed x15, local copies, waits for them, and re-layouts  9.85 us

profile of v1, /device:TPU:1, one launch (start us, length us, event | category | flops | bytes accessed | tf_op | source)
XLA Modules:
  0.0 64.2 jit_solution(17480602926926555043)
XLA Ops:
  0.6 0.7 %reshape.28.lens_ref = s32[4,1,1024]{2,1,0:T(1,128)S(1)} reshape(s32[4,1024]{1,0:T(4,128)} %bitcast.13) | data formatting | bytes 32768 | tf_op jit(solution)/shard_map/reshape | solution.py:366
  1.4 0.0 copy-start
  1.4 1.0 %copy-done = bf16[256,1024]{1,0:T(8,128)(2,1)S(1)} copy-done((bf16[256,1024]{1,0:T(8,128)(2,1)S(1)}, bf16[256,1024]{1,0:T(8,128)(2,1)}, u32[]{:S(2)}) %copy-start) | copy-done | bytes 524312
  2.4 0.0 copy-start.1
  2.4 0.9 %copy-done.1 = s32[1024,4,16]{0,2,1:T(8,128)S(1)} copy-done((s32[1024,4,16]{0,2,1:T(8,128)S(1)}, s32[1024,4,16]{0,2,1:T(8,128)}, u32[]{:S(2)}) %copy-start.1) | copy-done | bytes 262168
  3.4 0.0 copy-start.2
  3.4 0.7 %copy-done.2 = s32[1024]{0:T(1024)S(1)} copy-done((s32[1024]{0:T(1024)S(1)}, s32[1024]{0:T(1024)}, u32[]{:S(2)}) %copy-start.2) | copy-done | bytes 4120
  4.0 0.0 copy-start.3
  4.0 0.7 %copy-done.3 = f32[1024]{0:T(1024)S(1)} copy-done((f32[1024]{0:T(1024)S(1)}, f32[1024]{0:T(1024)}, u32[]{:S(2)}) %copy-start.3) | copy-done | bytes 4120
  4.7 0.0 copy-start.4
  4.7 0.7 %copy-done.4 = f32[1024]{0:T(1024)S(1)} copy-done((f32[1024]{0:T(1024)S(1)}, f32[1024]{0:T(1024)}, u32[]{:S(2)}) %copy-start.4) | copy-done | bytes 4120
  5.4 53.0 %shard_map.119 = (f32[4,512,256]{2,1,0:T(8,128)}, f32[16,256]{1,0:T(8,128)S(1)}, f32[256,1024]{1,0:T(8,128)S(1)}, f32[1,1024]{1,0:T(1,128)S(1)}, f32[1,1024]{1,0:T(1,128)S(1)}) custom-call(s32[4,16,1024]{2,1,0:T(8,128)S(1)} %bitcast.7, s32[4,1,1024]{2,1,0:T(1,128)S(1)} %reshape.28.lens_ref, s32[1,1024]{1,0:T(1,128)S(1)} %bitcast.10, ...), custom_call_target="tpu_custom_call" | custom-call | tf_op jit(solution)/shard_map/pallas_call | solution.py:370
  58.4 3.0 %copy.18 = f32[4,512,256]{2,1,0:T(8,128)} copy(f32[4,512,256]{2,1,0:T(8,128)} %get-tuple-element.20) | data formatting | bytes 4194304
  61.4 0.6 copy.19
  62.0 1.0 %copy.20 = f32[256,1024]{1,0:T(8,128)} copy(f32[256,1024]{1,0:T(8,128)S(1)} %get-tuple-element.22) | data formatting | bytes 2097152
  63.0 0.6 copy.21
  63.6 0.6 copy.22
Async XLA Ops:
  1.4 1.0 %copy-start = (bf16[256,1024]{1,0:T(8,128)(2,1)S(1)}, bf16[256,1024]{1,0:T(8,128)(2,1)}, u32[]{:S(2)}) copy-start(bf16[256,1024]{1,0:T(8,128)(2,1)} %hw_ref.1) | copy-start | bytes 1572868
  2.4 0.9 %copy-start.1 = (s32[1024,4,16]{0,2,1:T(8,128)S(1)}, s32[1024,4,16]{0,2,1:T(8,128)}, u32[]{:S(2)}) copy-start(s32[1024,4,16]{0,2,1:T(8,128)} %param.9) | copy-start | bytes 786436
  3.4 0.7 %copy-start.2 = (s32[1024]{0:T(1024)S(1)}, s32[1024]{0:T(1024)}, u32[]{:S(2)}) copy-start(s32[1024]{0:T(1024)} %param.11) | copy-start | bytes 12292
  4.0 0.7 %copy-start.3 = (f32[1024]{0:T(1024)S(1)}, f32[1024]{0:T(1024)}, u32[]{:S(2)}) copy-start(f32[1024]{0:T(1024)} %param.14) | copy-start | bytes 12292
  4.7 0.7 %copy-start.4 = (f32[1024]{0:T(1024)S(1)}, f32[1024]{0:T(1024)}, u32[]{:S(2)}) copy-start(f32[1024]{0:T(1024)} %param.15) | copy-start | bytes 12292

commit v2 on v1

v2 whole, which is shorter than its diff:
```python
import jax
import jax.numpy as jnp
from jax import lax
from jax.experimental import pallas as pl
from jax.experimental.pallas import tpu as pltpu
from jax.sharding import PartitionSpec as P

MESH = pl.DeviceIdType.MESH
BF = jnp.bfloat16
F32 = jnp.float32
NZ = 8
NP = 8
CH = 256


def mm(a, b):
    return lax.dot_general(a, b, (((1,), (0,)), ((), ())), preferred_element_type=F32)


def mm_nt(a, b):
    return lax.dot_general(a, b, (((1,), (1,)), ((), ())), preferred_element_type=F32)


def split_hi_lo(v):
    hi = v.astype(BF)
    return hi, (v - hi.astype(F32)).astype(BF)


def kernel(
    ids_hbm, lens_hbm, lab_hbm, hw_hbm, bias_hbm, ow_hbm, rows_hbm, pw_hbm,
    rg_hbm, proj_hbm, hr_hbm, vec_hbm,
    rg_ref, proj_ref, ids_ref, lens_ref, lab_ref, hw_ref, bias_ref, ow_ref, mid_ref, rows_ref,
    wc_ref, rt_ref, wct_ref, hwt_ref, bc_ref, oc_ref,
    cnt_ref, pool_ref, part_ref, ra_ref, sb_ref, rb_ref, pt_ref,
    gb_ref, act_ref, sl_ref, spt_ref, dpt_ref, dpool_ref,
    hs1_ref, hr1_ref, ps1_ref, pr1_ref, hs2_ref, hr2_ref, ps2_ref, pr2_ref,
    hs3_ref, hr3_ref, vs1_ref, vr1_ref, vs2_ref, vr2_ref, vs3_ref, vr3_ref,
    in_sem, out_sem, n_send, n_recv, a_send, a_recv, b_send, b_recv, c_send, c_recv,
    h1_send, h1_recv, p1_send, p1_recv, h2_send, h2_recv, p2_send, p2_recv,
    h3_send, h3_recv, h4_send, h4_recv,
    v1_send, v1_recv, v2_send, v2_recv, v3_send, v3_recv, v4_send, v4_recv,
):
    c = lax.axis_index("col")
    g = lax.axis_index("grp")
    h, k = c // 2, lax.rem(c, 2)
    p, z = g // NZ, lax.rem(g, NZ)
    tables, _, samples = ids_ref.shape
    bag = ids_ref.shape[1]
    row_total = rows_ref.shape[1]
    width = rows_ref.shape[2]
    hid = hw_ref.shape[1]
    n_ch = samples // CH

    core_peer = {"col": 2 * h + (1 - k), "grp": g}
    chip_peer = {"col": 2 * (1 - h) + k, "grp": g}

    def plane_peer(d):
        q = lax.rem(p + d, NP)
        return q, {"col": c, "grp": q * NZ + z}

    def z_peer(d):
        q = lax.rem(z + d, NZ)
        return q, {"col": c, "grp": p * NZ + q}

    def far_peer(d):
        e = lax.rem(h * NP + p + d, 2 * NP)
        qh, qp = e // NP, lax.rem(e, NP)
        return e, {"col": 2 * qh + k, "grp": qp * NZ + z}

    def rows_copy(t):
        return pltpu.make_async_copy(rows_hbm.at[t], rows_ref.at[t], in_sem.at[t])

    own_w = pw_hbm.at[pl.ds(pl.multiple_of(c * tables * width, 256), tables * width)]
    small = [
        pltpu.make_async_copy(src, dst, in_sem.at[tables + n])
        for n, (src, dst) in enumerate((
            (ids_hbm, ids_ref), (lens_hbm, lens_ref), (hw_hbm, hw_ref), (bias_hbm, bias_ref),
            (ow_hbm, ow_ref), (lab_hbm, lab_ref), (own_w, wc_ref)))
    ]
    for copy in small[:2]:
        copy.start()
    for t in range(tables):
        rows_copy(t).start()
    for copy in small[2:]:
        copy.start()

    barrier = pltpu.get_barrier_semaphore()
    pl.semaphore_signal(barrier, inc=1, device_id=core_peer, device_id_type=MESH)

    def greet_far(d, carry):
        pl.semaphore_signal(barrier, inc=1, device_id=far_peer(d)[1], device_id_type=MESH)
        return carry

    def greet_z(d, carry):
        pl.semaphore_signal(barrier, inc=1, device_id=z_peer(d)[1], device_id_type=MESH)
        return carry

    lax.fori_loop(1, 2 * NP, greet_far, 0)
    lax.fori_loop(1, NZ, greet_z, 0)

    def cols_of(j):
        return pl.ds(pl.multiple_of(j * CH, CH), CH)

    n_own = tables // 2

    def copy_n(j, i):
        t = k * n_own + i
        return pltpu.make_async_remote_copy(
            cnt_ref.at[j, t], cnt_ref.at[j, t], n_send.at[j * n_own + i], n_recv.at[j * n_own + i],
            device_id=core_peer, device_id_type=MESH)

    def wait_n(j, i):
        t = (1 - k) * n_own + i
        pltpu.make_async_remote_copy(
            cnt_ref.at[j, t], cnt_ref.at[j, t], n_send.at[j * n_own + i], n_recv.at[j * n_own + i],
            device_id=core_peer, device_id_type=MESH).wait_recv()

    def counts(j, send):
        lanes = CH // 128

        def block(n, carry):
            i, b = n // lanes, lax.rem(n, lanes)
            t = k * n_own + i
            ids = mid_ref[t, :, pl.ds(pl.multiple_of(j * CH + b * 128, 128), 128)]
            cols = pl.ds(pl.multiple_of(b * 128, 128), 128)
            spread = [jnp.broadcast_to(ids[q : q + 1], (16, 128)).astype(jnp.int16) for q in range(bag)]
            first = lax.broadcasted_iota(jnp.int32, (16, 128), 0).astype(jnp.int16)
            one, zero = jnp.ones((16, 128), BF), jnp.zeros((16, 128), BF)
            for r in range(row_total // 16):
                row = first + jnp.int16(r * 16)
                acc = jnp.where(spread[0] == row, one, zero)
                for q in range(1, bag):
                    acc = acc + jnp.where(spread[q] == row, one, zero)
                cnt_ref[j, t, r * 16 : (r + 1) * 16, cols] = acc
            if send:
                @pl.when(b == lanes - 1)
                def _():
                    copy_n(j, i).start()

            return carry

        lax.fori_loop(0, n_own * lanes, block, 0)

    def pool_block(j, t):
        ws = pl.ds(pl.multiple_of(t * width, width), width)
        both = mm(rt_ref[t], cnt_ref[j, t])
        pool_ref[ws, cols_of(j)] = (both[:width] + both[width:]).astype(BF)

    def pool_own(j):
        for i in range(n_own):
            pool_block(j, k * n_own + i)

    def pool_other(j):
        for i in range(n_own):
            wait_n(j, i)
            pool_block(j, (1 - k) * n_own + i)
        part_ref[j] = mm(wct_ref[...], pool_ref[:, cols_of(j)])
        copy_a(j).start()

    own_half = pl.ds(pl.multiple_of(k * 128, 128), 128)
    other_half = pl.ds(pl.multiple_of((1 - k) * 128, 128), 128)

    def copy_a(j):
        return pltpu.make_async_remote_copy(
            part_ref.at[j, other_half], ra_ref.at[j], a_send.at[j], a_recv.at[j],
            device_id=core_peer, device_id_type=MESH)

    def copy_b(j):
        return pltpu.make_async_remote_copy(
            sb_ref.at[j], rb_ref.at[j], b_send.at[j], b_recv.at[j],
            device_id=chip_peer, device_id_type=MESH)

    def copy_c(j):
        return pltpu.make_async_remote_copy(
            pt_ref.at[j, own_half], pt_ref.at[j, own_half], c_send.at[j], c_recv.at[j],
            device_id=core_peer, device_id_type=MESH)

    def wait_c(j):
        pltpu.make_async_remote_copy(
            pt_ref.at[j, other_half], pt_ref.at[j, other_half], c_send.at[j], c_recv.at[j],
            device_id=core_peer, device_id_type=MESH).wait_recv()

    def stage_b(j):
        copy_a(j).wait_recv()
        sb_ref[j] = (part_ref[j, own_half] + ra_ref[j]).astype(BF)
        copy_b(j).start()

    def stage_c(j):
        copy_b(j).wait_recv()
        pt_ref[j, own_half] = (sb_ref[j].astype(F32) + rb_ref[j].astype(F32)).astype(BF)
        copy_c(j).start()

    def mlp(j):
        wait_c(j)
        cols = cols_of(j)
        pt = pt_ref[j]
        logits = jnp.zeros((1, CH), F32)
        for q in range(hid // 256):
            hs = pl.ds(pl.multiple_of(lax.rem(c + q, hid // 256) * 256, 256), 256)
            bias = jnp.concatenate([bc_ref[hs, :]] * (CH // 128), axis=1)
            ow = jnp.concatenate([oc_ref[hs, :]] * (CH // 128), axis=1)
            pre = mm(hwt_ref[hs, :], pt) + bias
            sig = 0.5 * jnp.tanh(0.5 * pre) + 0.5
            act = pre * sig
            logits = logits + jnp.sum(act * ow, axis=0, keepdims=True)
            gb_ref[hs, cols] = (ow * (sig + act * (1.0 - sig))).astype(BF)
            if q == 0:
                act_ref[:, cols] = act.astype(BF)
        slopes = 0.5 * jnp.tanh(0.5 * logits) + 0.5 - lab_ref[:, cols].astype(F32)
        hi, lo = split_hi_lo(slopes)
        spot = lax.broadcasted_iota(jnp.int32, (16, CH), 0)
        sl_ref[:, cols] = jnp.where(
            spot == 0, hi.astype(F32), jnp.where(spot == 1, lo.astype(F32), 0.0)
        ).astype(BF)
        dpt_ref[:, cols] = (mm(hw_ref[...], gb_ref[:, cols]) * slopes).astype(BF)
        spt_ref[:, cols] = (pt.astype(F32) * slopes).astype(BF)

    small[0].wait()
    small[1].wait()
    for t in range(tables):
        spot = lax.broadcasted_iota(jnp.int32, (bag, samples), 0)
        mid_ref[t] = jnp.where(spot < lens_ref[t : t + 1, :], ids_ref[t], -1)
    counts(0, False)
    for t in range(tables):
        rows_copy(t).wait()
        hi, lo = split_hi_lo(rows_ref[t].T)
        rt_ref[t, :width] = hi
        rt_ref[t, width:] = lo
    small[6].wait()
    wct_ref[...] = wc_ref[...].T
    pl.semaphore_wait(barrier, 2 * NP + NZ - 1)
    for i in range(n_own):
        copy_n(0, i).start()
    pool_own(0)
    for j in range(1, n_ch):
        counts(j, True)
        if j >= 2:
            stage_b(j - 2)
        pool_other(j - 1)
        pool_own(j)
    stage_c(0)
    stage_b(n_ch - 2)
    pool_other(n_ch - 1)
    for copy in small[2:6]:
        copy.wait()
    hwt_ref[...] = hw_ref[...].T
    bc_ref[...] = jnp.broadcast_to(bias_ref[...], (128, hid)).T
    oc_ref[...] = jnp.broadcast_to(ow_ref[...], (128, hid)).T
    stage_b(n_ch - 1)
    mlp(0)
    for j in range(1, n_ch):
        stage_c(j)
        mlp(j)

    hs = pl.ds(pl.multiple_of(c * 256, 256), 256)
    g_own = gb_ref[hs, :]
    hgrad = mm_nt(spt_ref[...], g_own)
    brow = mm_nt(sl_ref[...], g_own)
    orow = mm_nt(sl_ref[...], act_ref[...])

    hs1_ref[...] = hgrad.astype(BF).reshape(NP, 32, 256)
    spot = lax.broadcasted_iota(jnp.int32, (8, 256), 0)
    vs1_ref[...] = jnp.where(
        spot == 0, brow[0:1] + brow[1:2], jnp.where(spot == 1, orow[0:1] + orow[1:2], 0.0))

    def h1_copy(q, dev):
        return pltpu.make_async_remote_copy(
            hs1_ref.at[q], hr1_ref.at[p], h1_send.at[q], h1_recv.at[p], device_id=dev, device_id_type=MESH)

    def p1_copy(q, dev):
        return pltpu.make_async_remote_copy(
            ps1_ref.at[q], pr1_ref.at[p], p1_send.at[q], p1_recv.at[p], device_id=dev, device_id_type=MESH)

    def h2_copy(q, dev):
        return pltpu.make_async_remote_copy(
            hs2_ref, hr2_ref.at[z], h2_send.at[q], h2_recv.at[z], device_id=dev, device_id_type=MESH)

    def p2_copy(q, dev):
        return pltpu.make_async_remote_copy(
            ps2_ref.at[q], pr2_ref.at[z], p2_send.at[q], p2_recv.at[z], device_id=dev, device_id_type=MESH)

    def h3_copy(e, dev):
        own = h * NP + p
        return pltpu.make_async_remote_copy(
            hs3_ref, hr3_ref.at[own], h3_send.at[e], h3_recv.at[own], device_id=dev, device_id_type=MESH)

    def v1_copy(dev):
        return pltpu.make_async_remote_copy(
            vs1_ref, vr1_ref.at[p], v1_send, v1_recv.at[p], device_id=dev, device_id_type=MESH)

    def v2_copy(q, dev):
        return pltpu.make_async_remote_copy(
            vs2_ref, vr2_ref.at[z], v2_send.at[q], v2_recv.at[z], device_id=dev, device_id_type=MESH)

    def v3_copy(e, dev):
        return pltpu.make_async_remote_copy(
            vs3_ref, vr3_ref.at[h], v3_send.at[e], v3_recv.at[h], device_id=dev, device_id_type=MESH)

    def v3_from(qh):
        return pltpu.make_async_remote_copy(
            vs3_ref, vr3_ref.at[qh], v3_send.at[0], v3_recv.at[qh],
            device_id={"col": 2 * qh + k, "grp": (2 * qh + k) * NZ + z}, device_id_type=MESH)

    vec_peer = {"col": c, "grp": c * NZ + z}

    def start_all(peer, copy, count):
        def go(d, carry):
            copy(*peer(d)).start()
            return carry

        lax.fori_loop(1, count, go, 0)

    def wait_all(peer, src, dst_slots, send, recv, count):
        def go(d, carry):
            q, dev = peer(d)
            pltpu.make_async_remote_copy(
                src(q), dst_slots.at[q], send.at[q], recv.at[q], device_id=dev, device_id_type=MESH).wait_recv()
            return carry

        lax.fori_loop(1, count, go, 0)

    def wait_sent(peer, copy, count):
        def go(d, carry):
            copy(*peer(d)).wait_send()
            return carry

        lax.fori_loop(1, count, go, 0)

    start_all(plane_peer, h1_copy, NP)

    @pl.when(p != c)
    def _():
        v1_copy(vec_peer).start()

    @pl.when(p == c)
    def _():
        vr1_ref[p] = vs1_ref[...]

    hr1_ref[p] = hs1_ref[p]

    for t in range(tables):
        pg = mm_nt(pool_ref[t * width : (t + 1) * width], dpt_ref[...])
        half = NP // tables
        for q in range(half):
            ps1_ref[t * half + q] = pg[q * 128 : (q + 1) * 128].astype(BF)
    start_all(plane_peer, p1_copy, NP)
    pr1_ref[p] = ps1_ref[p]

    def row_grad(t):
        ws = slice(t * width, (t + 1) * width)
        dpool_ref[ws] = mm(wc_ref[ws], dpt_ref[...]).astype(BF)
        acc = mm_nt(cnt_ref[0, t], dpool_ref[ws, :CH])
        for j in range(1, n_ch):
            acc = acc + mm_nt(cnt_ref[j, t], dpool_ref[ws, j * CH : (j + 1) * CH])
        rg_ref[t] = acc
        pltpu.make_async_copy(rg_ref.at[t], rg_hbm.at[t], out_sem.at[t]).start()

    def slot_sum(ref, rows):
        acc = ref[0, rows].astype(F32)
        for q in range(1, NP):
            acc = acc + ref[q, rows].astype(F32)
        return acc

    row_grad(0)

    wait_all(plane_peer, lambda q: hs1_ref.at[q], hr1_ref, h1_send, h1_recv, NP)
    hs2_ref[...] = slot_sum(hr1_ref, slice(0, 32)).astype(BF)
    start_all(z_peer, h2_copy, NZ)
    hr2_ref[z] = hs2_ref[...]

    @pl.when(p == c)
    def _():
        wait_all(plane_peer, lambda q: vs1_ref, vr1_ref, v2_send, v1_recv, NP)
        vs2_ref[...] = slot_sum(vr1_ref, slice(0, 8))
        start_all(z_peer, v2_copy, NZ)
        vr2_ref[z] = vs2_ref[...]

    row_grad(1)

    wait_all(plane_peer, lambda q: ps1_ref.at[q], pr1_ref, p1_send, p1_recv, NP)
    for q in range(NZ):
        ps2_ref[q] = slot_sum(pr1_ref, slice(q * 16, (q + 1) * 16)).astype(BF)
    start_all(z_peer, p2_copy, NZ)
    pr2_ref[z] = ps2_ref[z]

    wait_all(z_peer, lambda q: hs2_ref, hr2_ref, h2_send, h2_recv, NZ)
    hs3_ref[...] = slot_sum(hr2_ref, slice(0, 32)).astype(BF)
    start_all(far_peer, h3_copy, 2 * NP)
    hr3_ref[h * NP + p] = hs3_ref[...]

    @pl.when(p == c)
    def _():
        wait_all(z_peer, lambda q: vs2_ref, vr2_ref, v2_send, v2_recv, NZ)
        vs3_ref[...] = slot_sum(vr2_ref, slice(0, 8))
        start_all(far_peer, v3_copy, 2 * NP)
        vr3_ref[h] = vs3_ref[...]

    row_grad(2)
    row_grad(3)

    wait_all(z_peer, lambda q: ps2_ref.at[q], pr2_ref, p2_send, p2_recv, NZ)
    proj_ref[...] = slot_sum(pr2_ref, slice(0, 16))
    proj_out = pltpu.make_async_copy(proj_ref, proj_hbm, out_sem.at[tables])
    proj_out.start()

    wait_all(far_peer, lambda e: hs3_ref, hr3_ref, h3_send, h3_recv, 2 * NP)
    h4 = pltpu.make_async_remote_copy(
        hr3_ref, hr_hbm.at[k], h4_send, h4_recv, device_id=core_peer, device_id_type=MESH)
    h4.start()
    hr_out = pltpu.make_async_copy(hr3_ref, hr_hbm.at[k], out_sem.at[tables + 1])
    hr_out.start()
    for qh in range(2):
        @pl.when((h != qh) | (p != c))
        def _():
            v3_from(qh).wait_recv()

    v4 = pltpu.make_async_remote_copy(
        vr3_ref, vec_hbm.at[k], v4_send, v4_recv, device_id=core_peer, device_id_type=MESH)
    v4.start()
    vec_out = pltpu.make_async_copy(vr3_ref, vec_hbm.at[k], out_sem.at[tables + 2])
    vec_out.start()

    for j in range(n_ch):
        copy_a(j).wait_send()
        copy_b(j).wait_send()
        copy_c(j).wait_send()
        for i in range(n_own):
            copy_n(j, i).wait_send()
    wait_sent(plane_peer, h1_copy, NP)
    wait_sent(plane_peer, p1_copy, NP)
    wait_sent(z_peer, h2_copy, NZ)
    wait_sent(z_peer, p2_copy, NZ)
    wait_sent(far_peer, h3_copy, 2 * NP)
    for t in range(tables):
        pltpu.make_async_copy(rg_ref.at[t], rg_hbm.at[t], out_sem.at[t]).wait()
    @pl.when(p != c)
    def _():
        v1_copy(vec_peer).wait_send()

    @pl.when(p == c)
    def _():
        wait_sent(z_peer, v2_copy, NZ)
        wait_sent(far_peer, v3_copy, 2 * NP)

    proj_out.wait()
    hr_out.wait()
    vec_out.wait()
    h4.wait_send()
    v4.wait_send()
    pltpu.make_async_remote_copy(
        hr3_ref, hr_hbm.at[1 - k], h4_send, h4_recv, device_id=core_peer, device_id_type=MESH).wait_recv()
    pltpu.make_async_remote_copy(
        vr3_ref, vec_hbm.at[1 - k], v4_send, v4_recv, device_id=core_peer, device_id_type=MESH).wait_recv()


def write_out(
    rg_hbm, proj_hbm, hr_hbm, vec_hbm, rg_out, proj_out, hid_out, bg_out, og_out,
    rg_ref, proj_ref, hr_ref, vec_ref, hid_ref, bg_ref, og_ref, in_sem, out_sem,
):
    tables = rg_ref.shape[0]

    def copy(src, dst, sem):
        return pltpu.make_async_copy(src, dst, sem)

    ins = [copy(hr_hbm, hr_ref, in_sem.at[0]), copy(vec_hbm, vec_ref, in_sem.at[1]), copy(proj_hbm, proj_ref, in_sem.at[2])]
    ins += [copy(rg_hbm.at[t], rg_ref.at[t], in_sem.at[3 + t]) for t in range(tables)]
    outs = [copy(rg_ref.at[t], rg_out.at[t], out_sem.at[t]) for t in range(tables)]
    outs += [
        copy(src, dst, out_sem.at[tables + n])
        for n, (src, dst) in enumerate(((proj_ref, proj_out), (hid_ref, hid_out), (bg_ref, bg_out), (og_ref, og_out)))
    ]
    for one in ins:
        one.start()
    for one in ins[:3]:
        one.wait()
    for core in range(2):
        for qh in range(2):
            col = slice((2 * qh + core) * 256, (2 * qh + core + 1) * 256)
            for q in range(NP):
                hid_ref[q * 32 : (q + 1) * 32, col] = hr_ref[core, qh * NP + q].astype(F32)
            bg_ref[:, col] = vec_ref[core, qh, 0:1]
            og_ref[:, col] = vec_ref[core, qh, 1:2]
    for one in outs[tables:]:
        one.start()
    for t in range(tables):
        ins[3 + t].wait()
        outs[t].start()
    for one in outs:
        one.wait()


def body(rows, bag_ids, bag_lengths, labels, proj_weight, hidden_weight, hidden_bias, out_weight):
    tables, row_total, width = rows.shape
    samples, _, bag = bag_ids.shape
    feats, proj = proj_weight.shape
    hid = hidden_weight.shape[1]
    own = tables * width
    n_ch = samples // CH
    ids = bag_ids.transpose(1, 2, 0)
    lens = bag_lengths.T
    hbm = pl.BlockSpec(memory_space=pl.ANY)
    dma = pltpu.SemaphoreType.DMA
    out = pl.pallas_call(
        kernel,
        out_shape=(
            jax.ShapeDtypeStruct(rows.shape, F32),
            jax.ShapeDtypeStruct((feats // 256, proj), F32),
            jax.ShapeDtypeStruct((2, 2 * NP, 32, 256), BF),
            jax.ShapeDtypeStruct((2, 2, 8, 256), F32),
        ),
        in_specs=[hbm] * 8,
        out_specs=[hbm] * 4,
        scratch_shapes=[
            pltpu.VMEM(rows.shape, F32),
            pltpu.VMEM((feats // 256, proj), F32),
            pltpu.VMEM((tables, bag, samples), jnp.int32),
            pltpu.VMEM((tables, samples), jnp.int32),
            pltpu.VMEM((1, samples), jnp.int32),
            pltpu.VMEM((proj, hid), BF),
            pltpu.VMEM((1, hid), F32),
            pltpu.VMEM((1, hid), F32),
            pltpu.VMEM((tables, bag, samples), jnp.int32),
            pltpu.VMEM((tables, row_total, width), F32),
            pltpu.VMEM((own, proj), BF),
            pltpu.VMEM((tables, 2 * width, row_total), BF),
            pltpu.VMEM((proj, own), BF),
            pltpu.VMEM((hid, proj), BF),
            pltpu.VMEM((hid, 128), F32),
            pltpu.VMEM((hid, 128), F32),
            pltpu.VMEM((n_ch, tables, row_total, CH), BF),
            pltpu.VMEM((own, samples), BF),
            pltpu.VMEM((n_ch, proj, CH), F32),
            pltpu.VMEM((n_ch, proj // 2, CH), F32),
            pltpu.VMEM((n_ch, proj // 2, CH), BF),
            pltpu.VMEM((n_ch, proj // 2, CH), BF),
            pltpu.VMEM((n_ch, proj, CH), BF),
            pltpu.VMEM((hid, samples), BF),
            pltpu.VMEM((256, samples), BF),
            pltpu.VMEM((16, samples), BF),
            pltpu.VMEM((proj, samples), BF),
            pltpu.VMEM((proj, samples), BF),
            pltpu.VMEM((own, samples), BF),
            pltpu.VMEM((NP, 32, 256), BF),
            pltpu.VMEM((NP, 32, 256), BF),
            pltpu.VMEM((NP, 128, proj), BF),
            pltpu.VMEM((NP, 128, proj), BF),
            pltpu.VMEM((32, 256), BF),
            pltpu.VMEM((NZ, 32, 256), BF),
            pltpu.VMEM((NZ, 16, proj), BF),
            pltpu.VMEM((NZ, 16, proj), BF),
            pltpu.VMEM((32, 256), BF),
            pltpu.VMEM((2 * NP, 32, 256), BF),
            pltpu.VMEM((8, 256), F32),
            pltpu.VMEM((NP, 8, 256), F32),
            pltpu.VMEM((8, 256), F32),
            pltpu.VMEM((NZ, 8, 256), F32),
            pltpu.VMEM((8, 256), F32),
            pltpu.VMEM((2, 8, 256), F32),
            dma((tables + 7,)),
            dma((tables + 3,)),
            dma((n_ch * 2,)), dma((n_ch * 2,)),
            dma((n_ch,)), dma((n_ch,)), dma((n_ch,)), dma((n_ch,)), dma((n_ch,)), dma((n_ch,)),
            dma((NP,)), dma((NP,)), dma((NP,)), dma((NP,)),
            dma((NZ,)), dma((NZ,)), dma((NZ,)), dma((NZ,)),
            dma((2 * NP,)), dma((2 * NP,)),
            dma(()), dma(()),
            dma(()), dma((NP,)), dma((NZ,)), dma((NZ,)), dma((2 * NP,)), dma((2,)), dma(()), dma(()),
        ],
        compiler_params=pltpu.CompilerParams(
            collective_id=0, has_side_effects=True, vmem_limit_bytes=64 * 1024 * 1024
        ),
    )(
        ids, lens, labels.reshape(1, samples), hidden_weight, hidden_bias.reshape(1, hid),
        out_weight.reshape(1, hid), rows, proj_weight,
    )
    shapes = (
        jax.ShapeDtypeStruct(rows.shape, F32),
        jax.ShapeDtypeStruct((feats // 256, proj), F32),
        jax.ShapeDtypeStruct((proj, hid), F32),
        jax.ShapeDtypeStruct((1, hid), F32),
        jax.ShapeDtypeStruct((1, hid), F32),
    )
    held = [pltpu.VMEM(o.shape, o.dtype) for o in (*out, *shapes[2:])]
    out = pl.pallas_call(
        write_out,
        out_shape=shapes,
        in_specs=[hbm] * 4,
        out_specs=[hbm] * 5,
        scratch_shapes=held + [dma((tables + 3,)), dma((tables + 4,))],
        compiler_params=pltpu.CompilerParams(vmem_limit_bytes=64 * 1024 * 1024),
    )(*out)
    return out[0], out[1], out[2], out[3].reshape(hid), out[4].reshape(hid)


def solution(mesh):
    return jax.shard_map(
        body,
        mesh=mesh,
        in_specs=(
            P(None, "grp", "col"),
            P("grp", None, None),
            P("grp", None),
            P("grp"),
            P(),
            P(),
            P(),
            P(),
        ),
        out_specs=(P(None, "grp", "col"), P(("col", "grp"), None), P(), P(), P()),
        check_vma=False,
    )
```

time: 64.6 us -> 53.3 us (0.83)
  local copies, waits for them, and re-layouts: 10.6 us -> 0 us
    unnamed x15 -> x0, local copies, waits for them, and re-layouts: 9.85 us -> none
    pallas_call x1, Pallas kernels: 53 us -> 49.6 us  [body(): pl.pallas_call(kernel, out_shape=(jax.ShapeDtypeStruct(rows.shape, F32),...]
    pallas_call x0 -> x1, Pallas kernels: none -> 2.92 us  [body(): pl.pallas_call(write_out, out_shape=shapes, in_specs=[hbm] * 4, out_specs...]
    reshape x1 -> x0, local copies, waits for them, and re-layouts: 0.73 us -> none  [body(): lens = bag_lengths.T.reshape(tables, 1, samples)]
where the time goes in v2:
time: 53.3 us; the launch traced here: 53.2 us
  Pallas kernels  52.5 us (98%)
  between operations  0.64 us (1%)
    pallas_call x1, Pallas kernels, body(): pl.pallas_call(kernel, out_shape=(jax.ShapeDtypeStruct(rows.shape, F32),...  49.6 us
    pallas_call x1, Pallas kernels, body(): pl.pallas_call(write_out, out_shape=shapes, in_specs=[hbm] * 4, out_specs...  2.92 us

profile of v2, /device:TPU:1, one launch (start us, length us, event | category | flops | bytes accessed | tf_op | source)
XLA Modules:
  0.0 53.2 jit_solution(10137991051790553031)
XLA Ops:
  0.6 49.6 %shard_map.119 = (f32[4,512,256]{2,1,0:T(8,128)}, f32[16,256]{1,0:T(8,128)}, bf16[2,16,32,256]{3,2,1,0:T(8,128)(2,1)}, f32[2,2,8,256]{3,2,1,0:T(8,128)}) custom-call(s32[4,16,1024]{2,1,0:T(8,128)} %bitcast.7, s32[4,1024]{1,0:T(4,128)} %bitcast.8, s32[1,1024]{1,0:T(1,128)} %bitcast.9, bf16[256,1024]{1,0:T(8,128)(2,1)} %hw_hbm.1, f32[1,1024]{1,0:T(1,128)} %bitcast.10, ...), custom_call_target="tpu_custom_call" | custom-call | tf_op jit(solution)/shard_map/pallas_call | solution.py:503
  50.2 2.9 %shard_map.120 = (f32[4,512,256]{2,1,0:T(8,128)}, f32[16,256]{1,0:T(8,128)}, f32[256,1024]{1,0:T(8,128)}, f32[1,1024]{1,0:T(1,128)}, f32[1,1024]{1,0:T(1,128)}) custom-call(f32[4,512,256]{2,1,0:T(8,128)} %get-tuple-element.14.rg_hbm, f32[16,256]{1,0:T(8,128)} %get-tuple-element.15.proj_hbm, bf16[2,16,32,256]{3,2,1,0:T(8,128)(2,1)} %get-tuple-element.16.hr_hbm, ...), custom_call_target="tpu_custom_call" | custom-call | tf_op jit(solution)/shard_map/pallas_call | solution.py:584

commit v3 on v2

--- a/solution.py
+++ b/solution.py
@@ -31,8 +31,8 @@
     rg_hbm, proj_hbm, hr_hbm, vec_hbm,
     rg_ref, proj_ref, ids_ref, lens_ref, lab_ref, hw_ref, bias_ref, ow_ref, mid_ref, rows_ref,
     wc_ref, rt_ref, wct_ref, hwt_ref, bc_ref, oc_ref,
-    cnt_ref, pool_ref, part_ref, ra_ref, sb_ref, rb_ref, pt_ref,
-    gb_ref, act_ref, sl_ref, spt_ref, dpt_ref, dpool_ref,
+    cnt0_ref, cnt1_ref, cnt2_ref, cnt3_ref, pool_ref, part_ref, ra_ref, sb_ref, rb_ref, pt_ref,
+    gb_ref, hacc_ref, oacc_ref, dpt_ref, dpool_ref,
     hs1_ref, hr1_ref, ps1_ref, pr1_ref, hs2_ref, hr2_ref, ps2_ref, pr2_ref,
     hs3_ref, hr3_ref, vs1_ref, vr1_ref, vs2_ref, vr2_ref, vs3_ref, vr3_ref,
     in_sem, out_sem, n_send, n_recv, a_send, a_recv, b_send, b_recv, c_send, c_recv,
@@ -49,23 +49,33 @@
     row_total = rows_ref.shape[1]
     width = rows_ref.shape[2]
     hid = hw_ref.shape[1]
-    n_ch = samples // CH
+    cnts = (cnt0_ref, cnt1_ref, cnt2_ref, cnt3_ref)
+    n_ch = len(cnts)
 
     core_peer = {"col": 2 * h + (1 - k), "grp": g}
     chip_peer = {"col": 2 * (1 - h) + k, "grp": g}
 
+    y, x_lo = p // 2, lax.rem(p, 2)
+    plane_steps = ((2, 1), (1, 1), (3, 1), (2, 0), (0, 1), (1, 0), (3, 0))
+    far_steps = sorted(
+        ((dy, dx) for dy in range(4) for dx in range(4) if dy or dx), key=lambda s: -min(s[0], 4 - s[0]) - min(s[1], 4 - s[1])
+    )
+    z_steps = (4, 3, 5, 2, 6, 1, 7)
+
     def plane_peer(d):
-        q = lax.rem(p + d, NP)
+        dy, dx = plane_steps[d]
+        q = lax.rem(y + dy, 4) * 2 + lax.rem(x_lo + dx, 2)
         return q, {"col": c, "grp": q * NZ + z}
 
     def z_peer(d):
-        q = lax.rem(z + d, NZ)
+        q = lax.rem(z + z_steps[d], NZ)
         return q, {"col": c, "grp": p * NZ + q}
 
     def far_peer(d):
-        e = lax.rem(h * NP + p + d, 2 * NP)
-        qh, qp = e // NP, lax.rem(e, NP)
-        return e, {"col": 2 * qh + k, "grp": qp * NZ + z}
+        dy, dx = far_steps[d]
+        qx = lax.rem(h * 2 + x_lo + dx, 4)
+        qh, qp = qx // 2, lax.rem(y + dy, 4) * 2 + lax.rem(qx, 2)
+        return qh * NP + qp, {"col": 2 * qh + k, "grp": qp * NZ + z}
 
     def rows_copy(t):
         return pltpu.make_async_copy(rows_hbm.at[t], rows_ref.at[t], in_sem.at[t])
@@ -87,16 +97,10 @@
     barrier = pltpu.get_barrier_semaphore()
     pl.semaphore_signal(barrier, inc=1, device_id=core_peer, device_id_type=MESH)
 
-    def greet_far(d, carry):
+    for d in range(2 * NP - 1):
         pl.semaphore_signal(barrier, inc=1, device_id=far_peer(d)[1], device_id_type=MESH)
-        return carry
-
-    def greet_z(d, carry):
+    for d in range(NZ - 1):
         pl.semaphore_signal(barrier, inc=1, device_id=z_peer(d)[1], device_id_type=MESH)
-        return carry
-
-    lax.fori_loop(1, 2 * NP, greet_far, 0)
-    lax.fori_loop(1, NZ, greet_z, 0)
 
     def cols_of(j):
         return pl.ds(pl.multiple_of(j * CH, CH), CH)
@@ -106,54 +110,65 @@
     def copy_n(j, i):
         t = k * n_own + i
         return pltpu.make_async_remote_copy(
-            cnt_ref.at[j, t], cnt_ref.at[j, t], n_send.at[j * n_own + i], n_recv.at[j * n_own + i],
+            cnts[j].at[t], cnts[j].at[t], n_send.at[j * n_own + i], n_recv.at[j * n_own + i],
             device_id=core_peer, device_id_type=MESH)
 
     def wait_n(j, i):
         t = (1 - k) * n_own + i
         pltpu.make_async_remote_copy(
-            cnt_ref.at[j, t], cnt_ref.at[j, t], n_send.at[j * n_own + i], n_recv.at[j * n_own + i],
+            cnts[j].at[t], cnts[j].at[t], n_send.at[j * n_own + i], n_recv.at[j * n_own + i],
             device_id=core_peer, device_id_type=MESH).wait_recv()
 
-    def counts(j, send):
-        lanes = CH // 128
-
-        def block(n, carry):
-            i, b = n // lanes, lax.rem(n, lanes)
-            t = k * n_own + i
-            ids = mid_ref[t, :, pl.ds(pl.multiple_of(j * CH + b * 128, 128), 128)]
-            cols = pl.ds(pl.multiple_of(b * 128, 128), 128)
-            spread = [jnp.broadcast_to(ids[q : q + 1], (16, 128)).astype(jnp.int16) for q in range(bag)]
-            first = lax.broadcasted_iota(jnp.int32, (16, 128), 0).astype(jnp.int16)
-            one, zero = jnp.ones((16, 128), BF), jnp.zeros((16, 128), BF)
-            for r in range(row_total // 16):
-                row = first + jnp.int16(r * 16)
-                acc = jnp.where(spread[0] == row, one, zero)
-                for q in range(1, bag):
-                    acc = acc + jnp.where(spread[q] == row, one, zero)
-                cnt_ref[j, t, r * 16 : (r + 1) * 16, cols] = acc
-            if send:
-                @pl.when(b == lanes - 1)
-                def _():
-                    copy_n(j, i).start()
-
-            return carry
-
-        lax.fori_loop(0, n_own * lanes, block, 0)
+    lanes = CH // 128
+
+    def count_block(j, n):
+        i, b = n // lanes, lax.rem(n, lanes)
+        t = k * n_own + i
+        ids = mid_ref[t, :, pl.ds(pl.multiple_of(j * CH + b * 128, 128), 128)]
+        cols = pl.ds(pl.multiple_of(b * 128, 128), 128)
+        spread = [jnp.broadcast_to(ids[q : q + 1], (16, 128)).astype(jnp.int16) for q in range(bag)]
+        first = lax.broadcasted_iota(jnp.int32, (16, 128), 0).astype(jnp.int16)
+        one, zero = jnp.ones((16, 128), BF), jnp.zeros((16, 128), BF)
+        for r in range(row_total // 16):
+            row = first + jnp.int16(r * 16)
+            acc = jnp.where(spread[0] == row, one, zero)
+            for q in range(1, bag):
+                acc = acc + jnp.where(spread[q] == row, one, zero)
+            cnts[j][t, r * 16 : (r + 1) * 16, cols] = acc
 
     def pool_block(j, t):
         ws = pl.ds(pl.multiple_of(t * width, width), width)
-        both = mm(rt_ref[t], cnt_ref[j, t])
+        both = mm(rt_ref[t], cnts[j][t])
         pool_ref[ws, cols_of(j)] = (both[:width] + both[width:]).astype(BF)
 
-    def pool_own(j):
-        for i in range(n_own):
-            pool_block(j, k * n_own + i)
-
-    def pool_other(j):
-        for i in range(n_own):
-            wait_n(j, i)
-            pool_block(j, (1 - k) * n_own + i)
+    def pool_own(j, i):
+        pool_block(j, k * n_own + i)
+
+    def pool_other(j, i):
+        pool_block(j, (1 - k) * n_own + i)
+
+    def counts_pool(j, own, other):
+        def first(n, carry):
+            pool_own(own, n)
+            count_block(j, n)
+            return carry
+
+        def second(n, carry):
+            if other is not None:
+                pool_other(other, n - lanes)
+            count_block(j, n)
+            return carry
+
+        lax.fori_loop(0, lanes, first, 0)
+        if other is not None:
+            copy_n(j, 0).start()
+            for i in range(n_own):
+                wait_n(other, i)
+        lax.fori_loop(lanes, 2 * lanes, second, 0)
+        if other is not None:
+            copy_n(j, 1).start()
+
+    def project(j):
         part_ref[j] = mm(wct_ref[...], pool_ref[:, cols_of(j)])
         copy_a(j).start()
 
@@ -205,22 +220,32 @@
             logits = logits + jnp.sum(act * ow, axis=0, keepdims=True)
             gb_ref[hs, cols] = (ow * (sig + act * (1.0 - sig))).astype(BF)
             if q == 0:
-                act_ref[:, cols] = act.astype(BF)
+                act_own = act.astype(BF)
         slopes = 0.5 * jnp.tanh(0.5 * logits) + 0.5 - lab_ref[:, cols].astype(F32)
         hi, lo = split_hi_lo(slopes)
         spot = lax.broadcasted_iota(jnp.int32, (16, CH), 0)
-        sl_ref[:, cols] = jnp.where(
+        slope_rows = jnp.where(
             spot == 0, hi.astype(F32), jnp.where(spot == 1, lo.astype(F32), 0.0)
         ).astype(BF)
         dpt_ref[:, cols] = (mm(hw_ref[...], gb_ref[:, cols]) * slopes).astype(BF)
-        spt_ref[:, cols] = (pt.astype(F32) * slopes).astype(BF)
+        g_own = gb_ref[pl.ds(pl.multiple_of(c * 256, 256), 256), cols]
+        sp = (pt.astype(F32) * slopes).astype(BF)
+        h_term = mm_nt(jnp.concatenate([sp, slope_rows], axis=0), g_own)
+        o_term = mm_nt(slope_rows, act_own)
+        hacc_ref[...] = h_term if j == 0 else hacc_ref[...] + h_term
+        oacc_ref[...] = o_term if j == 0 else oacc_ref[...] + o_term
 
     small[0].wait()
     small[1].wait()
     for t in range(tables):
         spot = lax.broadcasted_iota(jnp.int32, (bag, samples), 0)
         mid_ref[t] = jnp.where(spot < lens_ref[t : t + 1, :], ids_ref[t], -1)
-    counts(0, False)
+
+    def first_counts(n, carry):
+        count_block(0, n)
+        return carry
+
+    lax.fori_loop(0, n_own * lanes, first_counts, 0)
     for t in range(tables):
         rows_copy(t).wait()
         hi, lo = split_hi_lo(rows_ref[t].T)
@@ -228,37 +253,45 @@
         rt_ref[t, width:] = lo
     small[6].wait()
     wct_ref[...] = wc_ref[...].T
+    counts_pool(1, 0, None)
     pl.semaphore_wait(barrier, 2 * NP + NZ - 1)
+    for j in range(2):
+        for i in range(n_own):
+            copy_n(j, i).start()
+    counts_pool(2, 1, 0)
+    project(0)
+    counts_pool(3, 2, 1)
+    project(1)
     for i in range(n_own):
-        copy_n(0, i).start()
-    pool_own(0)
-    for j in range(1, n_ch):
-        counts(j, True)
-        if j >= 2:
-            stage_b(j - 2)
-        pool_other(j - 1)
-        pool_own(j)
-    stage_c(0)
-    stage_b(n_ch - 2)
-    pool_other(n_ch - 1)
+        wait_n(2, i)
+        pool_other(2, i)
+    project(2)
+    stage_b(0)
+    for i in range(n_own):
+        pool_own(3, i)
+    stage_b(1)
+    for i in range(n_own):
+        wait_n(3, i)
+        pool_other(3, i)
+    project(3)
+    stage_b(2)
     for copy in small[2:6]:
         copy.wait()
     hwt_ref[...] = hw_ref[...].T
     bc_ref[...] = jnp.broadcast_to(bias_ref[...], (128, hid)).T
     oc_ref[...] = jnp.broadcast_to(ow_ref[...], (128, hid)).T
-    stage_b(n_ch - 1)
+    stage_b(3)
+    stage_c(0)
+    stage_c(1)
     mlp(0)
-    for j in range(1, n_ch):
-        stage_c(j)
-        mlp(j)
-
-    hs = pl.ds(pl.multiple_of(c * 256, 256), 256)
-    g_own = gb_ref[hs, :]
-    hgrad = mm_nt(spt_ref[...], g_own)
-    brow = mm_nt(sl_ref[...], g_own)
-    orow = mm_nt(sl_ref[...], act_ref[...])
-
-    hs1_ref[...] = hgrad.astype(BF).reshape(NP, 32, 256)
+    mlp(1)
+    stage_c(2)
+    stage_c(3)
+    mlp(2)
+    mlp(3)
+
+    hs1_ref[...] = hacc_ref[: hw_ref.shape[0]].astype(BF).reshape(NP, 32, 256)
+    brow, orow = hacc_ref[hw_ref.shape[0] :], oacc_ref[...]
     spot = lax.broadcasted_iota(jnp.int32, (8, 256), 0)
     vs1_ref[...] = jnp.where(
         spot == 0, brow[0:1] + brow[1:2], jnp.where(spot == 1, orow[0:1] + orow[1:2], 0.0))
@@ -304,27 +337,18 @@
     vec_peer = {"col": c, "grp": c * NZ + z}
 
     def start_all(peer, copy, count):
-        def go(d, carry):
+        for d in range(count - 1):
             copy(*peer(d)).start()
-            return carry
-
-        lax.fori_loop(1, count, go, 0)
 
     def wait_all(peer, src, dst_slots, send, recv, count):
-        def go(d, carry):
+        for d in range(count - 1):
             q, dev = peer(d)
             pltpu.make_async_remote_copy(
                 src(q), dst_slots.at[q], send.at[q], recv.at[q], device_id=dev, device_id_type=MESH).wait_recv()
-            return carry
-
-        lax.fori_loop(1, count, go, 0)
 
     def wait_sent(peer, copy, count):
-        def go(d, carry):
+        for d in range(count - 1):
             copy(*peer(d)).wait_send()
-            return carry
-
-        lax.fori_loop(1, count, go, 0)
 
     start_all(plane_peer, h1_copy, NP)
 
@@ -349,9 +373,9 @@
     def row_grad(t):
         ws = slice(t * width, (t + 1) * width)
         dpool_ref[ws] = mm(wc_ref[ws], dpt_ref[...]).astype(BF)
-        acc = mm_nt(cnt_ref[0, t], dpool_ref[ws, :CH])
+        acc = mm_nt(cnts[0][t], dpool_ref[ws, :CH])
         for j in range(1, n_ch):
-            acc = acc + mm_nt(cnt_ref[j, t], dpool_ref[ws, j * CH : (j + 1) * CH])
+            acc = acc + mm_nt(cnts[j][t], dpool_ref[ws, j * CH : (j + 1) * CH])
         rg_ref[t] = acc
         pltpu.make_async_copy(rg_ref.at[t], rg_hbm.at[t], out_sem.at[t]).start()
 
@@ -527,7 +551,7 @@
             pltpu.VMEM((hid, proj), BF),
             pltpu.VMEM((hid, 128), F32),
             pltpu.VMEM((hid, 128), F32),
-            pltpu.VMEM((n_ch, tables, row_total, CH), BF),
+            *[pltpu.VMEM((tables, row_total, CH), BF)] * n_ch,
             pltpu.VMEM((own, samples), BF),
             pltpu.VMEM((n_ch, proj, CH), F32),
             pltpu.VMEM((n_ch, proj // 2, CH), F32),
@@ -535,9 +559,8 @@
             pltpu.VMEM((n_ch, proj // 2, CH), BF),
             pltpu.VMEM((n_ch, proj, CH), BF),
             pltpu.VMEM((hid, samples), BF),
-            pltpu.VMEM((256, samples), BF),
-            pltpu.VMEM((16, samples), BF),
-            pltpu.VMEM((proj, samples), BF),
+            pltpu.VMEM((proj + 16, 256), F32),
+            pltpu.VMEM((16, 256), F32),
             pltpu.VMEM((proj, samples), BF),
             pltpu.VMEM((own, samples), BF),
             pltpu.VMEM((NP, 32, 256), BF),

time: 53.3 us -> 50.9 us (0.955)
  Pallas kernels: 52.5 us -> 50.1 us
    pallas_call x1, Pallas kernels: 49.6 us -> 47.2 us  [body(): pl.pallas_call(kernel, out_shape=(jax.ShapeDtypeStruct(rows.shape, F32),...]
where the time goes in v3:
time: 50.9 us; the launch traced here: 50.8 us
  Pallas kernels  50.1 us (98%)
  between operations  0.64 us (1%)
    pallas_call x1, Pallas kernels, body(): pl.pallas_call(kernel, out_shape=(jax.ShapeDtypeStruct(rows.shape, F32),...  47.2 us
    pallas_call x1, Pallas kernels, body(): pl.pallas_call(write_out, out_shape=shapes, in_specs=[hbm] * 4, out_specs...  2.92 us

profile of v3, /device:TPU:1, one launch (start us, length us, event | category | flops | bytes accessed | tf_op | source)
XLA Modules:
  0.0 50.8 jit_solution(17065198090706429589)
XLA Ops:
  0.6 47.2 %shard_map.119 = (f32[4,512,256]{2,1,0:T(8,128)}, f32[16,256]{1,0:T(8,128)}, bf16[2,16,32,256]{3,2,1,0:T(8,128)(2,1)}, f32[2,2,8,256]{3,2,1,0:T(8,128)}) custom-call(s32[4,16,1024]{2,1,0:T(8,128)} %bitcast.7, s32[4,1024]{1,0:T(4,128)} %bitcast.8, s32[1,1024]{1,0:T(1,128)} %bitcast.9, bf16[256,1024]{1,0:T(8,128)(2,1)} %hw_hbm.1, f32[1,1024]{1,0:T(1,128)} %bitcast.10, ...), custom_call_target="tpu_custom_call" | custom-call | tf_op jit(solution)/shard_map/pallas_call | solution.py:527
  47.8 2.9 %shard_map.120 = (f32[4,512,256]{2,1,0:T(8,128)}, f32[16,256]{1,0:T(8,128)}, f32[256,1024]{1,0:T(8,128)}, f32[1,1024]{1,0:T(1,128)}, f32[1,1024]{1,0:T(1,128)}) custom-call(f32[4,512,256]{2,1,0:T(8,128)} %get-tuple-element.14.rg_hbm, f32[16,256]{1,0:T(8,128)} %get-tuple-element.15.proj_hbm, bf16[2,16,32,256]{3,2,1,0:T(8,128)(2,1)} %get-tuple-element.16.hr_hbm, ...), custom_call_target="tpu_custom_call" | custom-call | tf_op jit(solution)/shard_map/pallas_call | solution.py:607
